TPU v7x, 256 devices: a whole 4x4x8 slice. The times are simulated.
256 devices in a mesh: win: 16 (over x_hi, z), atom: 16 (over x_lo, y, core).
Axes of the slice: x: 4 (x_hi: 2, x_lo: 2; x = x_hi * 2 + x_lo), y: 4, z: 8, core: 2. Of those that a mesh axis runs over, the one named last changes fastest.
Arguments:
- retarded: bfloat16 [512, 32, 2, 128, 128], P(('win', 'atom')), may hold values from -0.375 to 0.375
- sigma_in: bfloat16 [512, 32, 2, 128, 128], P(('win', 'atom')), may hold values from -6 to 6
- bit_shifts: int32 [3], replicated, may hold values from 0 to 3, as said below
- occupation: float32 [3], replicated, may hold values from 0.3 to 3
- neighbors: int32 [32, 3], replicated, may hold values from 0 to 31, as said below
- coupling: bfloat16 [3, 128, 128], replicated, may hold values from -0.375 to 0.375
Outputs:
- self_energy: bfloat16 [512, 32, 2, 128, 128], P('win', 'atom')
Inputs may be any that keep to these rules, and one draw needn't show every extreme that they name: `bit_shifts`: three different values; among them are 0 and 3, in an order drawn afresh. `neighbors`: column 0 of row b is b itself; the other columns of row b lie within b - 1 to b + 1.
All inputs are finite; a program needn't handle non-finite values.
Results may differ from a plain program's by a relative error of at most 0.007.
Values may be sent and summed in bfloat16 or wider, within the bound.
A program may use at most 128 MiB of HBM per device.

v0:
```python
import jax
import jax.numpy as jnp
from jax import lax
from jax.sharding import PartitionSpec as P


def partner(value, axis, distance):
    mask = 2**distance
    pairs = [(source, source ^ mask) for source in range(lax.axis_size(axis))]
    return lax.ppermute(value, axis, pairs)


def extended(cells, sides, width):
    for axis, dim in sides:
        count = lax.axis_size(axis)
        ends = count - 1
        head = lax.slice_in_dim(cells, 0, width, axis=dim)
        tail = lax.slice_in_dim(cells, cells.shape[dim] - width, cells.shape[dim], axis=dim)
        cells = jnp.concatenate(
            [
                lax.ppermute(tail, axis, [(i, (i + 1) % count) for i in range(ends)]),
                cells,
                lax.ppermute(head, axis, [((i + 1) % count, i) for i in range(ends)]),
            ],
            axis=dim,
        )
    return cells


def complex_product(left, right, form):
    real_part = jnp.einsum(
        form, left[:, :, 0], right[:, :, 0], preferred_element_type=jnp.float32
    ) - jnp.einsum(form, left[:, :, 1], right[:, :, 1], preferred_element_type=jnp.float32)
    imag_part = jnp.einsum(
        form, left[:, :, 0], right[:, :, 1], preferred_element_type=jnp.float32
    ) + jnp.einsum(form, left[:, :, 1], right[:, :, 0], preferred_element_type=jnp.float32)
    return jnp.stack([real_part, imag_part], axis=2).astype(jnp.bfloat16)


def partner_sum(lesser, bit_shifts, occupation):
    bit_count = lax.axis_size("win").bit_length() - 1
    summed = jnp.zeros(lesser.shape, jnp.float32)
    for bit_number in range(bit_count):
        weight = jnp.sum(jnp.where(bit_shifts == bit_number, occupation, 0.0))
        arrived = partner(lesser, "win", bit_number)
        summed = summed + weight * arrived.astype(jnp.float32)
    return summed.astype(jnp.bfloat16)


def couple(source, indices, coupling):
    directions = coupling.shape[0]
    picks = [jnp.take(source, indices[:, direction], axis=1) for direction in range(directions)]
    result = jnp.zeros(picks[0].shape, jnp.float32)
    for direction in range(directions):
        bent = jnp.einsum(
            "ij,erxjk->erxik",
            coupling[direction],
            picks[direction],
            preferred_element_type=jnp.float32,
        ).astype(jnp.bfloat16)
        result = result + jnp.einsum(
            "erxij,kj->erxik", bent, coupling[direction], preferred_element_type=jnp.float32
        )
    return result.astype(jnp.bfloat16)


def on_device(retarded, sigma_in, bit_shifts, occupation, neighbors, coupling):
    product = complex_product(retarded, sigma_in, "ebij,ebjk->ebik")
    lesser = complex_product(product, retarded, "ebij,ebkj->ebik")
    regrouped = lax.all_to_all(lesser, "atom", split_axis=1, concat_axis=0, tiled=True)
    partners = partner_sum(regrouped, bit_shifts, occupation)
    widened = extended(partners, (("atom", 1),), 1)
    owned = partners.shape[1]
    first_block = lax.axis_index("atom") * owned
    own_rows = lax.dynamic_slice_in_dim(neighbors, first_block, owned, 0)
    return couple(widened, own_rows - first_block + 1, coupling)


def solution(mesh):
    return jax.shard_map(
        on_device,
        mesh=mesh,
        in_specs=(
            P(("win", "atom"), None, None, None, None),
            P(("win", "atom"), None, None, None, None),
            P(),
            P(),
            P(),
            P(),
        ),
        out_specs=P("win", "atom", None, None, None),
        check_vma=False,
    )
```

profile of v0, /device:TPU:25, one launch (start us, length us, event | category | flops | bytes accessed | tf_op | source)
XLA Modules:
  0.0 556.8 jit_solution(7877296545857997896)
XLA Ops:
  0.0 3.1 fusion.40
  3.5 1.3 copy-done.2
  4.7 0.7 fusion.31
  5.4 0.8 subtract_convert_fusion.1
  6.3 1.6 fusion.44
  7.9 1.6 fusion.34
  9.4 0.8 add_convert_fusion.3
  10.3 1.6 fusion.51
  11.8 1.6 fusion.54
  13.8 0.6 copy.16
  14.4 53.9 %all_to_all.18 = bf16[2,32,2,128,128]{4,3,0,2,1:T(8,128)(2,1)S(1)} all-to-all(bf16[2,32,2,128,128]{4,3,0,2,1:T(8,128)(2,1)S(1)} %copy.16), channel_id=1, replica_groups=mesh['win'=16,'atom'=16] {'atom'}, dimensions={1} | all-to-all | bytes 8388608 | tf_op jit(solution)/shard_map/all_to_all | solution.py:70
  68.3 0.6 copy.17
  68.9 1.7 collective-permute-start
  70.6 3.0 collective-permute-start.1
  73.6 4.2 collective-permute-start.2
  77.8 2.5 collective-permute-start.3
  80.3 0.7 fusion.77
  81.0 170.0 %collective-permute-done = bf16[32,2,2,128,128]{4,3,2,1,0:T(8,128)(2,1)S(1)} collective-permute-done((bf16[32,2,2,128,128]{4,3,2,1,0:T(8,128)(2,1)S(1)}, bf16[32,2,2,128,128]{4,3,2,1,0:T(8,128)(2,1)S(1)}, u32[]{:S(2)}, u32[]{:S(2)}) %collective-permute-start) | collective-permute-done | bytes 4194336 | tf_op jit(solution)/shard_map/ppermute | solution.py:10
  251.0 185.8 %collective-permute-done.2 = bf16[32,2,2,128,128]{4,3,2,1,0:T(8,128)(2,1)S(1)} collective-permute-done((bf16[32,2,2,128,128]{4,3,2,1,0:T(8,128)(2,1)S(1)}, bf16[32,2,2,128,128]{4,3,2,1,0:T(8,128)(2,1)S(1)}, u32[]{:S(2)}, u32[]{:S(2)}) %collective-permute-start.2) | collective-permute-done | bytes 4194336 | tf_op jit(solution)/shard_map/ppermute | solution.py:10
  436.8 7.2 %add_convert_fusion.1 = bf16[32,2,2,128,128]{4,3,2,1,0:T(8,128)(2,1)S(1)} fusion(bf16[32,2,2,128,128]{4,3,2,1,0:T(8,128)(2,1)S(1)} %collective-permute-done.3, bf16[32,2,2,128,128]{4,3,2,1,0:T(8,128)(2,1)S(1)} %collective-permute-done.2, bf16[32,2,2,128,128]{4,3,2,1,0:T(8,128)(2,1)S(1)} %collective-permute-done.1, ...), kind=kLoop, calls=%fused_computation.8 | loop fusion | flops 25165824 | bytes 20971536 | tf_op jit(solution)/shard_map/convert_element_type | solution.py:47
  444.0 1.9 fusion.84
  445.9 0.8 copy-done.1
  446.6 4.3 collective-permute-start.4
  451.0 1.9 collective-permute-start.5
  453.0 21.2 %collective-permute-done.4 = bf16[32,1,2,128,128]{4,3,2,1,0:T(8,128)(2,1)} collective-permute-done((bf16[32,1,2,128,128]{4,3,2,1,0:T(8,128)(2,1)}, bf16[32,1,2,128,128]{4,3,2,1,0:T(8,128)(2,1)}, u32[]{:S(2)}, u32[]{:S(2)}) %collective-permute-start.4) | collective-permute-done | bytes 2097184 | tf_op jit(solution)/shard_map/ppermute | solution.py:21
  474.3 6.3 %collective-permute-done.5 = bf16[32,1,2,128,128]{4,3,2,1,0:T(8,128)(2,1)} collective-permute-done((bf16[32,1,2,128,128]{4,3,2,1,0:T(8,128)(2,1)S(1)}, bf16[32,1,2,128,128]{4,3,2,1,0:T(8,128)(2,1)}, u32[]{:S(2)}, u32[]{:S(2)}) %collective-permute-start.5) | collective-permute-done | bytes 2097184 | tf_op jit(solution)/shard_map/ppermute | solution.py:23
  480.6 7.1 %pad_maximum_fusion = bf16[32,4,2,128,128]{4,3,2,1,0:T(8,128)(2,1)} fusion(bf16[32,1,2,128,128]{4,3,2,1,0:T(8,128)(2,1)} %collective-permute-done.5, bf16[32,2,2,128,128]{4,3,2,1,0:T(8,128)(2,1)} %copy-done.1, bf16[32,1,2,128,128]{4,3,2,1,0:T(8,128)(2,1)} %collective-permute-done.4), kind=kLoop, calls=%fused_computation.6 | loop fusion | flops 8388608 | bytes 16777216 | tf_op jit(solution)/shard_map/concatenate | solution.py:19
  487.7 3.1 broadcast.71.clone.1
  490.7 9.0 %while.7 = (s32[]{:T(128)}, bf16[32,4,2,128,128]{4,3,2,1,0:T(8,128)(2,1)}, s32[2,1]{0,1:T(1,128)S(1)}, bf16[2,32,2,128,128]{4,3,2,1,0:T(8,128)(2,1)}, s32[]{:T(128)}) while((s32[]{:T(128)}, bf16[32,4,2,128,128]{4,3,2,1,0:T(8,128)(2,1)}, s32[2,1]{0,1:T(1,128)S(1)}, bf16[2,32,2,128,128]{4,3,2,1,0:T(8,128)(2,1)}, s32[]{:T(128)}) %tuple.52), condition=%wide.while_cond.clone, body=%wide.while_body.clone.sunk | while | flops 2 | bytes 4195401 | solution.py:52
  490.7 0.6 constant_dynamic-slice_fusion.7
  491.4 3.8 bitcast_dynamic-update-slice_fusion.7
  495.2 0.6 constant_dynamic-slice_fusion.7
  495.9 3.8 bitcast_dynamic-update-slice_fusion.7
  499.7 3.0 broadcast.71.clone
  502.7 8.6 %while.8 = (s32[]{:T(128)}, bf16[32,4,2,128,128]{4,3,2,1,0:T(8,128)(2,1)}, s32[2,1]{0,1:T(1,128)S(1)}, bf16[2,32,2,128,128]{4,3,2,1,0:T(8,128)(2,1)}, s32[]{:T(128)}) while((s32[]{:T(128)}, bf16[32,4,2,128,128]{4,3,2,1,0:T(8,128)(2,1)}, s32[2,1]{0,1:T(1,128)S(1)}, bf16[2,32,2,128,128]{4,3,2,1,0:T(8,128)(2,1)}, s32[]{:T(128)}) %tuple.58), condition=%wide.while_cond.clone.1, body=%wide.while_body.clone.1.sunk | while | flops 2 | bytes 4195401 | solution.py:52
  502.7 0.6 constant_dynamic-slice_fusion.8
  503.3 3.8 bitcast_dynamic-update-slice_fusion.8
  507.6 3.7 bitcast_dynamic-update-slice_fusion.8
  511.3 7.6 %select_bitcast_fusion = (bf16[32,2,2,128,128]{4,3,2,0,1:T(8,128)(2,1)}, bf16[32,2,2,128,128]{4,3,2,0,1:T(8,128)(2,1)}) fusion(bf16[2,32,2,128,128]{4,3,2,1,0:T(8,128)(2,1)} %get-tuple-element.28, pred[2]{0:T(512)(128)(4,1)S(1)} %get-tuple-element.60, bf16[2,32,2,128,128]{4,3,2,1,0:T(8,128)(2,1)} %get-tuple-element.27, pred[2]{0:T(512)(128)(4,1)S(1)} %get-tuple-element.61), kind=kLoop, calls=%fused_computation.22 | loop fusion | flops 4194304 | bytes 16777220 | tf_op jit(solution)/shard_map/jit(_take)/select_n | solution.py:52
  519.0 7.8 %fusion = f32[32,2,2,128,128]{4,3,2,1,0:T(8,128)} fusion(bf16[32,2,2,128,128]{4,3,2,0,1:T(8,128)(2,1)} %get-tuple-element.65, bf16[3,128,128]{2,1,0:T(8,128)(2,1)S(1)} %copy-done.3), kind=kOutput, calls=%fused_computation.10 | convolution fusion | flops 1075838976 | bytes 12648448 | tf_op jit(solution)/shard_map/erxij,kj->erxik/dot_general | solution.py:61
  526.7 7.7 %fusion.2 = f32[32,2,2,128,128]{4,3,2,1,0:T(8,128)} fusion(bf16[32,2,2,128,128]{4,3,2,0,1:T(8,128)(2,1)} %get-tuple-element.66, bf16[3,128,128]{2,1,0:T(8,128)(2,1)S(1)} %copy-done.3), kind=kOutput, calls=%fused_computation.12 | convolution fusion | flops 1075838976 | bytes 12648448 | tf_op jit(solution)/shard_map/erxij,kj->erxik/dot_general | solution.py:61
  534.5 3.0 broadcast.71.clone.2
  537.5 8.9 %while.6 = (s32[]{:T(128)}, bf16[32,4,2,128,128]{4,3,2,1,0:T(8,128)(2,1)}, s32[2,1]{0,1:T(1,128)S(1)}, bf16[2,32,2,128,128]{4,3,2,1,0:T(8,128)(2,1)}, s32[]{:T(128)}) while((s32[]{:T(128)}, bf16[32,4,2,128,128]{4,3,2,1,0:T(8,128)(2,1)}, s32[2,1]{0,1:T(1,128)S(1)}, bf16[2,32,2,128,128]{4,3,2,1,0:T(8,128)(2,1)}, s32[]{:T(128)}) %tuple.59), condition=%wide.while_cond, body=%wide.while_body.sunk | while | flops 2 | bytes 4195401 | solution.py:52
  537.5 0.6 constant_dynamic-slice_fusion.6
  538.1 3.9 bitcast_dynamic-update-slice_fusion.6
  541.9 0.6 constant_dynamic-slice_fusion.6
  542.5 3.8 bitcast_dynamic-update-slice_fusion.6
  546.4 10.4 %add_convert_fusion = bf16[32,2,2,128,128]{4,3,2,1,0:T(8,128)(2,1)} fusion(f32[32,2,2,128,128]{4,3,2,1,0:T(8,128)} %fusion, f32[32,2,2,128,128]{4,3,2,1,0:T(8,128)} %fusion.2, bf16[3,128,128]{2,1,0:T(8,128)(2,1)S(1)} %copy-done.3, bf16[2,32,2,128,128]{4,3,2,1,0:T(8,128)(2,1)} %get-tuple-element.26, pred[2]{0:T(512)(128)(4,1)S(1)} %get-tuple-element.59), kind=kOutput, calls=%fused_computation.7 | convolution fusion | flops 1084227584 | bytes 25231872 | tf_op jit(solution)/shard_map/erxij,kj->erxik/dot_general | solution.py:61
  (19 shorter events, 1.4 us)
Async XLA Ops:
  0.0 3.5 copy-start
  0.0 4.7 copy-start.2
  68.3 12.0 %copy-start.5 = (f32[3]{0:T(128)S(1)}, f32[3]{0:T(128)}, u32[]{:S(2)}) copy-start(f32[3]{0:T(128)} %param.11) | copy-start | bytes 40
  68.3 12.0 %copy-start.6 = (s32[3]{0:T(128)S(1)}, s32[3]{0:T(128)}, u32[]{:S(2)}) copy-start(s32[3]{0:T(128)} %param.10) | copy-start | bytes 40
  68.9 182.1 %collective-permute-start = (bf16[32,2,2,128,128]{4,3,2,1,0:T(8,128)(2,1)S(1)}, bf16[32,2,2,128,128]{4,3,2,1,0:T(8,128)(2,1)S(1)}, u32[]{:S(2)}, u32[]{:S(2)}) collective-permute-start(bf16[32,2,2,128,128]{4,3,2,1,0:T(8,128)(2,1)S(1)} %bitcast.142), channel_id=1, source_target_pairs={{0,16},{16,0},{32,48},{48,32},{64,80},{80,64},{96,112},{112,96},{1... | collective-permute-start | bytes 12582920 | tf_op jit(solution)/shard_map/ppermute | solution.py:10
  70.6 180.4 %collective-permute-start.1 = (bf16[32,2,2,128,128]{4,3,2,1,0:T(8,128)(2,1)S(1)}, bf16[32,2,2,128,128]{4,3,2,1,0:T(8,128)(2,1)S(1)}, u32[]{:S(2)}, u32[]{:S(2)}) collective-permute-start(bf16[32,2,2,128,128]{4,3,2,1,0:T(8,128)(2,1)S(1)} %bitcast.143), channel_id=1, source_target_pairs={{0,32},{16,48},{32,0},{48,16},{64,96},{80,112},{96,64},{112,80},{1... | collective-permute-start | bytes 12582920 | tf_op jit(solution)/shard_map/ppermute | solution.py:10
  73.6 363.2 %collective-permute-start.2 = (bf16[32,2,2,128,128]{4,3,2,1,0:T(8,128)(2,1)S(1)}, bf16[32,2,2,128,128]{4,3,2,1,0:T(8,128)(2,1)S(1)}, u32[]{:S(2)}, u32[]{:S(2)}) collective-permute-start(bf16[32,2,2,128,128]{4,3,2,1,0:T(8,128)(2,1)S(1)} %bitcast.144), channel_id=1, source_target_pairs={{0,64},{16,80},{32,96},{48,112},{64,0},{80,16},{96,32},{112,48},{1... | collective-permute-start | bytes 12582920 | tf_op jit(solution)/shard_map/ppermute | solution.py:10
  77.8 359.0 %collective-permute-start.3 = (bf16[32,2,2,128,128]{4,3,2,1,0:T(8,128)(2,1)S(1)}, bf16[32,2,2,128,128]{4,3,2,1,0:T(8,128)(2,1)S(1)}, u32[]{:S(2)}, u32[]{:S(2)}) collective-permute-start(bf16[32,2,2,128,128]{4,3,2,1,0:T(8,128)(2,1)S(1)} %bitcast.145), channel_id=1, source_target_pairs={{0,128},{16,144},{32,160},{48,176},{64,192},{80,208},{96,224},{112... | collective-permute-start | bytes 12582920 | tf_op jit(solution)/shard_map/ppermute | solution.py:10
  444.0 2.6 copy-start.1
  444.0 8.9 %copy-start.4 = (s32[32,3]{0,1:T(4,128)S(1)}, s32[32,3]{0,1:T(4,128)}, u32[]{:S(2)}) copy-start(s32[32,3]{0,1:T(4,128)} %param.12) | copy-start | bytes 1156
  446.6 27.6 %collective-permute-start.4 = (bf16[32,1,2,128,128]{4,3,2,1,0:T(8,128)(2,1)}, bf16[32,1,2,128,128]{4,3,2,1,0:T(8,128)(2,1)}, u32[]{:S(2)}, u32[]{:S(2)}) collective-permute-start(bf16[32,1,2,128,128]{4,3,2,1,0:T(8,128)(2,1)} %get-tuple-element.57), channel_id=1, source_target_pairs={{0,1},{1,2},{2,3},{3,4},{4,5},{5,6},{6,7},{7,8},{8,9},{9,10},{10,1... | collective-permute-start | bytes 6291464 | tf_op jit(solution)/shard_map/ppermute | solution.py:21
  451.0 29.6 %collective-permute-start.5 = (bf16[32,1,2,128,128]{4,3,2,1,0:T(8,128)(2,1)S(1)}, bf16[32,1,2,128,128]{4,3,2,1,0:T(8,128)(2,1)}, u32[]{:S(2)}, u32[]{:S(2)}) collective-permute-start(bf16[32,1,2,128,128]{4,3,2,1,0:T(8,128)(2,1)S(1)} %get-tuple-element.58), channel_id=1, source_target_pairs={{1,0},{2,1},{3,2},{4,3},{5,4},{6,5},{7,6},{8,7},{9,8},{10,9},{11,1... | collective-permute-start | bytes 6291464 | tf_op jit(solution)/shard_map/ppermute | solution.py:23
  511.3 7.6 %copy-start.3 = (bf16[3,128,128]{2,1,0:T(8,128)(2,1)S(1)}, bf16[3,128,128]{2,1,0:T(8,128)(2,1)}, u32[]{:S(2)}) copy-start(bf16[3,128,128]{2,1,0:T(8,128)(2,1)} %param.13) | copy-start | bytes 294916
where the time goes:
time: 557 us
  waiting for transfers between devices  383 us (69%)
  blocking collectives  53.9 us (10%)
  local copies, waits for them, and re-layouts  41 us (7%)
  matrix products  37.7 us (7%)
  other arithmetic  23.1 us (4%)
  starting transfers between devices  17.7 us (3%)
    ppermute x4, waiting for transfers between devices, partner(): return lax.ppermute(value, axis, pairs)  356 us
    all_to_all x1, blocking collectives, on_device(): lax.all_to_all(lesser, 'atom', split_axis=1, concat_axis=0, tiled=True)  53.9 us
    another operation x15, local copies, waits for them, and re-layouts, couple(): jnp.take(source, indices[:, direction], axis=1)  35.5 us
    dot_general x3, matrix products, couple(): jnp.einsum('erxij,kj->erxik', bent, coupling[direction], preferred_elemen...  25.9 us
    ppermute x1, waiting for transfers between devices, extended(): lax.ppermute(tail, axis, [(i, (i + 1) % count) for i in range(ends)])  21.2 us
    ppermute x4, starting transfers between devices, partner(): return lax.ppermute(value, axis, pairs)  11.4 us
  transfers between devices with their start and end apart: 6, of which 4 were waited for; matrix products, arithmetic and copies ran while one was open for 0% of the time, Pallas kernels for 0%

commit v1 on v0

v1 whole, which is shorter than its diff:
```python
import functools

import jax
import jax.numpy as jnp
from jax import lax
from jax.experimental import pallas as pl
from jax.experimental.pallas import tpu as pltpu
from jax.sharding import PartitionSpec as P

MESH = pl.DeviceIdType.MESH
F32 = jnp.float32
BF16 = jnp.bfloat16


def dot(left, right, contract):
    return lax.dot_general(left, right, ((contract[0:1], contract[1:2]), ((), ())), preferred_element_type=F32)


def fold(quad, norb):
    real = quad[:norb, :norb] - quad[norb:, norb:]
    imag = quad[:norb, norb:] + quad[norb:, :norb]
    return jnp.concatenate([real, imag], axis=0).astype(BF16)


def flip(win, bit):
    mask = 2**bit
    return win + mask * (1 - 2 * ((win // mask) % 2))


def kernel(
    bits,
    n_atom,
    shifts_ref,
    occ_ref,
    near_ref,
    green_hbm,
    sigma_hbm,
    coupling_ref,
    out_ref,
    green,
    sigma,
    lesser,
    part,
    got,
    total,
    in_sem,
    send_sem,
    recv_sem,
    give_sem,
    take_sem,
    own_sem,
):
    steps = n_atom
    own_e = green.shape[0]
    own_b = lesser.shape[1] // n_atom
    norb = green.shape[-1]
    win = lax.axis_index("win")
    atom = lax.axis_index("atom")
    partners = [flip(win, bit) for bit in bits]

    def owner(step):
        return lax.rem(atom + 1 + step, n_atom)

    def load(kind, j):
        source, target = ((green_hbm, green), (sigma_hbm, sigma))[kind]
        rows = pl.ds(j * own_b, own_b)
        return pltpu.make_async_copy(source.at[:, rows], target.at[:, rows], in_sem.at[kind, j])

    @pl.loop(0, n_atom)
    def _(i):
        j = lax.rem(atom + i, n_atom)
        load(0, j).start()
        load(1, j).start()

    barrier = pltpu.get_barrier_semaphore()
    for partner in partners:
        pl.semaphore_signal(barrier, inc=1, device_id=(partner, atom), device_id_type=MESH)

    @pl.loop(1, n_atom)
    def _(i):
        pl.semaphore_signal(barrier, inc=1, device_id=(win, lax.rem(atom + i, n_atom)), device_id_type=MESH)

    def make_lesser(j):
        load(0, j).wait()
        load(1, j).wait()
        for i in range(own_b):
            for e in range(own_e):
                b = j * own_b + i
                g = green[e, b].reshape(2 * norb, norb)
                s = jnp.concatenate([sigma[e, b, 0], sigma[e, b, 1]], axis=1)
                product = fold(dot(g, s, (1, 0)), norb)
                lesser[e, b] = fold(dot(product, g, (1, 1)), norb).reshape(2, norb, norb)

    directions = coupling_ref.shape[0]
    out_right = [coupling_ref[d] for d in range(directions)]

    def make_part(step, j):
        for i in range(own_b):
            bent = []
            for d in range(directions):
                n = near_ref[j * own_b + i, d]
                tiles = []
                for e in range(own_e):
                    picked = lesser[e, n]
                    tiles += [picked[0], picked[1]]
                wide = dot(out_right[d], jnp.concatenate(tiles, axis=1), (1, 0)).astype(BF16)
                bent.append(
                    jnp.concatenate([wide[:, t * norb : (t + 1) * norb] for t in range(2 * own_e)], axis=0)
                )
            full = dot(jnp.concatenate(bent, axis=1), jnp.concatenate(out_right, axis=1), (1, 1)).astype(BF16)
            for e in range(own_e):
                part[step, e, i] = full[2 * e * norb : 2 * (e + 1) * norb].reshape(2, norb, norb)

    def send(k, step):
        return pltpu.make_async_remote_copy(
            src_ref=part.at[step],
            dst_ref=got.at[k, step],
            send_sem=send_sem.at[k, step],
            recv_sem=recv_sem.at[k, step],
            device_id=(partners[k], atom),
            device_id_type=MESH,
        )

    def give(step):
        return pltpu.make_async_remote_copy(
            src_ref=total.at[step],
            dst_ref=out_ref.at[pl.ds(atom * own_e, own_e)],
            send_sem=give_sem.at[step],
            recv_sem=take_sem.at[step],
            device_id=(win, owner(step)),
            device_id_type=MESH,
        )

    make_lesser(atom)
    make_lesser(lax.rem(atom + 1, n_atom))
    pl.semaphore_wait(barrier, len(bits) + n_atom - 1)

    @pl.loop(0, steps)
    def _(step):
        @pl.when(step < steps - 2)
        def _():
            make_lesser(lax.rem(atom + 2 + step, n_atom))

        make_part(step, owner(step))
        for k in range(len(bits)):
            send(k, step).start()

    weights = []
    for bit in bits:
        weight = jnp.float32(0.0)
        for mode in range(shifts_ref.shape[0]):
            weight = weight + jnp.where(shifts_ref[mode] == bit, occ_ref[mode], 0.0)
        weights.append(weight)

    def add_up(step):
        for k in range(len(bits)):
            send(k, step).wait_recv()
        for e in range(own_e):
            for i in range(own_b):
                summed = weights[0] * got[0, step, e, i].astype(F32)
                for k in range(1, len(bits)):
                    summed = summed + weights[k] * got[k, step, e, i].astype(F32)
                total[step, e, i] = summed.astype(BF16)

    @pl.loop(0, steps - 1)
    def _(step):
        add_up(step)
        give(step).start()

    add_up(steps - 1)
    own = pltpu.make_async_copy(total.at[steps - 1], out_ref.at[pl.ds(atom * own_e, own_e)], own_sem)
    own.start()

    @pl.loop(0, steps - 1)
    def _(step):
        give(step).wait()

    @pl.loop(0, steps)
    def _(step):
        for k in range(len(bits)):
            send(k, step).wait_send()

    own.wait()


def call(bits, n_atom, retarded, sigma_in, bit_shifts, occupation, neighbors, coupling):
    own_e, blocks, _, norb, _ = retarded.shape
    own_b = blocks // n_atom
    piece = (own_e, own_b, 2, norb, norb)
    count = len(bits)
    smem = pl.BlockSpec(memory_space=pltpu.SMEM)
    hbm = pl.BlockSpec(memory_space=pl.ANY)
    return pl.pallas_call(
        functools.partial(kernel, bits, n_atom),
        out_shape=jax.ShapeDtypeStruct((own_e * n_atom, own_b, 2, norb, norb), BF16),
        in_specs=[smem, smem, smem, hbm, hbm, pl.BlockSpec(memory_space=pltpu.VMEM)],
        out_specs=hbm,
        scratch_shapes=[
            pltpu.VMEM(retarded.shape, BF16),
            pltpu.VMEM(retarded.shape, BF16),
            pltpu.VMEM(retarded.shape, BF16),
            pltpu.VMEM((n_atom, *piece), BF16),
            pltpu.VMEM((count, n_atom, *piece), BF16),
            pltpu.VMEM((n_atom, *piece), BF16),
            pltpu.SemaphoreType.DMA((2, n_atom)),
            pltpu.SemaphoreType.DMA((count, n_atom)),
            pltpu.SemaphoreType.DMA((count, n_atom)),
            pltpu.SemaphoreType.DMA((n_atom,)),
            pltpu.SemaphoreType.DMA((n_atom,)),
            pltpu.SemaphoreType.DMA(()),
        ],
        compiler_params=pltpu.CompilerParams(
            collective_id=bits[1], has_side_effects=True, vmem_limit_bytes=50 * 2**20
        ),
        name="self_energy",
    )(bit_shifts, occupation, neighbors, retarded, sigma_in, coupling)


def on_device(retarded, sigma_in, bit_shifts, occupation, neighbors, coupling):
    n_atom = lax.axis_size("atom")
    top = lax.axis_size("win").bit_length() - 2
    return lax.cond(
        jnp.any(bit_shifts == 1),
        functools.partial(call, (0, 1, top), n_atom),
        functools.partial(call, (0, 2, top), n_atom),
        retarded,
        sigma_in,
        bit_shifts,
        occupation,
        neighbors,
        coupling,
    )


def solution(mesh):
    return jax.shard_map(
        on_device,
        mesh=mesh,
        in_specs=(
            P(("win", "atom"), None, None, None, None),
            P(("win", "atom"), None, None, None, None),
            P(),
            P(),
            P(),
            P(),
        ),
        out_specs=P("win", "atom", None, None, None),
        check_vma=False,
    )
```

time: 557 us -> 198 us (0.36)
  the two profiles are of different devices: /device:TPU:25 before, /device:TPU:32 now
where the time goes in v1:
time: 198 us
  Pallas kernels  193 us (97%)
  local copies, waits for them, and re-layouts  2.78 us (1%)
    pallas_call x1, Pallas kernels, call(): pl.pallas_call(functools.partial(kernel, bits, n_atom), out_shape=jax.Sha...  193 us

profile of v1, /device:TPU:32, one launch (start us, length us, event | category | flops | bytes accessed | tf_op | source)
XLA Modules:
  0.0 197.9 jit_solution(973136611702509006)
XLA Ops:
  0.0 1.3 compare_reduce_fusion
  1.9 193.9 %conditional.1 = (bf16[32,2,2,128,128]{4,3,2,1,0:T(8,128)(2,1)S(1)}) conditional(s32[]{:T(128)} %convert_element_type.3, (s32[3]{0:T(128)}, f32[3]{0:T(128)}, s32[32,3]{0,1:T(4,128)}, bf16[2,32,2,128,128]{4,3,2,1,0:T(8,128)(2,1)}, bf16[2,32,2,128,128]{4,3,2,1,0:T(8,128)(2,1)}, /*index=5*/bf16[3,128,128]{2,1,0:T(8,128)(2,1)}) %tuple.11, (s32[3]{0:T(128)}, ...), branch_computations={%region_1.0_spmd, %region_2.0_spmd} | conditional | bytes 776 | solution.py:222
  2.0 0.8 copy.10.near_ref
  2.7 193.1 %self_energy.3 = bf16[32,2,2,128,128]{4,3,2,1,0:T(8,128)(2,1)S(1)} custom-call(s32[3]{0:T(128)} %get-tuple-element.38.shifts_ref, f32[3]{0:T(128)} %get-tuple-element.39.occ_ref, s32[32,3]{1,0:T(8,128)S(1)} %copy.10.near_ref, bf16[2,32,2,128,128]{4,3,2,1,0:T(8,128)(2,1)} %get-tuple-element.41.green_hbm, ...), custom_call_target="tpu_custom_call" | custom-call | tf_op jit(solution)/shard_map/cond/branch_1_fun/self_energy/pallas_call | solution.py:193
  195.8 2.0 %copy.14 = bf16[32,2,2,128,128]{4,3,2,1,0:T(8,128)(2,1)} copy(bf16[32,2,2,128,128]{4,3,2,1,0:T(8,128)(2,1)S(1)} %get-tuple-element.44) | data formatting | bytes 8388608

commit v2 on v1

v2 whole, which is shorter than its diff:
```python
import functools

import jax
import jax.numpy as jnp
from jax import lax
from jax.experimental import pallas as pl
from jax.experimental.pallas import tpu as pltpu
from jax.sharding import PartitionSpec as P

MESH = pl.DeviceIdType.MESH
F32 = jnp.float32
BF16 = jnp.bfloat16
LAG = 3


def dot(left, right, contract):
    return lax.dot_general(left, right, ((contract[0:1], contract[1:2]), ((), ())), preferred_element_type=F32)


def fold(quad, norb):
    real = quad[:norb, :norb] - quad[norb:, norb:]
    imag = quad[:norb, norb:] + quad[norb:, :norb]
    return jnp.concatenate([real, imag], axis=0).astype(BF16)


def flip(win, bit):
    mask = 2**bit
    return win + mask * (1 - 2 * ((win // mask) % 2))


class Context:
    def __init__(self, bits, n_atom, refs):
        (
            self.shifts,
            self.occ,
            self.near,
            self.green_hbm,
            self.sigma_hbm,
            self.coupling,
            self.out,
            self.green,
            self.sigma,
            self.lesser,
            self.part,
            self.total,
            self.in_sem,
            self.give_sem,
            self.take_sem,
            self.own_sem,
        ) = refs
        self.bits = bits
        self.n_atom = n_atom
        self.own_e = self.green.shape[0]
        self.own_b = self.lesser.shape[1] // n_atom
        self.norb = self.green.shape[-1]
        self.win = lax.axis_index("win")
        self.atom = lax.axis_index("atom")

    def owner(self, step):
        return lax.rem(self.atom + 1 + step, self.n_atom)

    def load(self, kind, j):
        source, target = ((self.green_hbm, self.green), (self.sigma_hbm, self.sigma))[kind]
        rows = pl.ds(j * self.own_b, self.own_b)
        return pltpu.make_async_copy(source.at[:, rows], target.at[:, rows], self.in_sem.at[kind, j])

    def greet(self, partners):
        barrier = pltpu.get_barrier_semaphore()
        for partner in partners:
            pl.semaphore_signal(barrier, inc=1, device_id=(partner, self.atom), device_id_type=MESH)

        @pl.loop(1, self.n_atom)
        def _(i):
            peer = lax.rem(self.atom + i, self.n_atom)
            pl.semaphore_signal(barrier, inc=1, device_id=(self.win, peer), device_id_type=MESH)

        return barrier

    def start_loads(self):
        @pl.loop(0, self.n_atom)
        def _(i):
            j = lax.rem(self.atom + i, self.n_atom)
            self.load(0, j).start()
            self.load(1, j).start()

    def make_lesser(self, j):
        self.load(0, j).wait()
        self.load(1, j).wait()
        norb = self.norb
        for i in range(self.own_b):
            for e in range(self.own_e):
                b = j * self.own_b + i
                g = self.green[e, b].reshape(2 * norb, norb)
                s = jnp.concatenate([self.sigma[e, b, 0], self.sigma[e, b, 1]], axis=1)
                product = fold(dot(g, s, (1, 0)), norb)
                self.lesser[e, b] = fold(dot(product, g, (1, 1)), norb).reshape(2, norb, norb)

    def make_part(self, step):
        norb, own_e = self.norb, self.own_e
        j = self.owner(step)
        matrices = [self.coupling[d] for d in range(self.coupling.shape[0])]
        for i in range(self.own_b):
            bent = []
            for d, matrix in enumerate(matrices):
                n = self.near[j * self.own_b + i, d]
                tiles = []
                for e in range(own_e):
                    picked = self.lesser[e, n]
                    tiles += [picked[0], picked[1]]
                wide = dot(matrix, jnp.concatenate(tiles, axis=1), (1, 0)).astype(BF16)
                bent.append(
                    jnp.concatenate([wide[:, t * norb : (t + 1) * norb] for t in range(2 * own_e)], axis=0)
                )
            full = dot(jnp.concatenate(bent, axis=1), jnp.concatenate(matrices, axis=1), (1, 1)).astype(BF16)
            for e in range(own_e):
                self.part[step, e, i] = full[2 * e * norb : 2 * (e + 1) * norb].reshape(2, norb, norb)

    def make_parts(self, barrier, waits, send_part):
        steps = self.n_atom
        self.make_lesser(self.atom)
        self.make_lesser(lax.rem(self.atom + 1, self.n_atom))
        pl.semaphore_wait(barrier, waits + self.n_atom - 1)

        @pl.loop(0, steps)
        def _(step):
            @pl.when(step < steps - 2)
            def _():
                self.make_lesser(lax.rem(self.atom + 2 + step, self.n_atom))

            self.make_part(step)
            send_part(step)

    def weights(self):
        weights = []
        for bit in self.bits:
            weight = jnp.float32(0.0)
            for mode in range(self.shifts.shape[0]):
                weight = weight + jnp.where(self.shifts[mode] == bit, self.occ[mode], 0.0)
            weights.append(weight)
        return weights

    def give(self, step):
        return pltpu.make_async_remote_copy(
            src_ref=self.total.at[step],
            dst_ref=self.out.at[pl.ds(self.atom * self.own_e, self.own_e)],
            send_sem=self.give_sem.at[step],
            recv_sem=self.take_sem.at[step],
            device_id=(self.win, self.owner(step)),
            device_id_type=MESH,
        )

    def keep(self):
        last = self.n_atom - 1
        rows = pl.ds(self.atom * self.own_e, self.own_e)
        return pltpu.make_async_copy(self.total.at[last], self.out.at[rows], self.own_sem)

    def finish(self):
        @pl.loop(0, self.n_atom - 1)
        def _(step):
            self.give(step).wait()

        self.keep().wait()


def near_kernel(bits, n_atom, *refs):
    here = Context(bits, n_atom, refs[:16])
    got, send_sem, recv_sem = refs[16:]
    partners = [flip(here.win, bit) for bit in bits]
    count, steps = len(bits), n_atom

    def send(k, step):
        return pltpu.make_async_remote_copy(
            src_ref=here.part.at[step],
            dst_ref=got.at[k, step],
            send_sem=send_sem.at[k, step],
            recv_sem=recv_sem.at[k, step],
            device_id=(partners[k], here.atom),
            device_id_type=MESH,
        )

    def send_part(step):
        for k in range(count):
            send(k, step).start()

    here.start_loads()
    barrier = here.greet(partners)
    here.make_parts(barrier, count, send_part)
    weights = here.weights()

    def add_up(step):
        for k in range(count):
            send(k, step).wait_recv()
        for e in range(here.own_e):
            for i in range(here.own_b):
                summed = weights[0] * got[0, step, e, i].astype(F32)
                for k in range(1, count):
                    summed = summed + weights[k] * got[k, step, e, i].astype(F32)
                here.total[step, e, i] = summed.astype(BF16)

    @pl.loop(0, steps - 1)
    def _(step):
        add_up(step)
        here.give(step).start()

    add_up(steps - 1)
    here.keep().start()

    @pl.loop(0, steps)
    def _(step):
        for k in range(count):
            send(k, step).wait_send()

    here.finish()


def far_kernel(bits, n_atom, *refs):
    here = Context(bits, n_atom, refs[:16])
    got_first, got_away, got_on, got_sum, got_top, mixed, half_send, half_recv, top_send, top_recv = refs[16:]
    steps = n_atom
    half = here.own_e // 2
    lead, rest = pl.ds(0, half), pl.ds(half, half)
    twin = flip(here.win, bits[0])
    cross = flip(twin, bits[1])
    across = flip(here.win, bits[2])

    def hop(kind, step):
        source, target, win = (
            (here.part.at[step, lead], got_first.at[step], twin),
            (here.part.at[step, rest], got_away.at[step], cross),
            (got_first.at[step], got_on.at[step], cross),
            (mixed.at[step], got_sum.at[step], twin),
        )[kind]
        return pltpu.make_async_remote_copy(
            src_ref=source,
            dst_ref=target,
            send_sem=half_send.at[kind, step],
            recv_sem=half_recv.at[kind, step],
            device_id=(win, here.atom),
            device_id_type=MESH,
        )

    def top(step):
        return pltpu.make_async_remote_copy(
            src_ref=here.part.at[step],
            dst_ref=got_top.at[step],
            send_sem=top_send.at[step],
            recv_sem=top_recv.at[step],
            device_id=(across, here.atom),
            device_id_type=MESH,
        )

    def send_part(step):
        hop(0, step).start()
        hop(1, step).start()
        top(step).start()

    here.start_loads()
    barrier = here.greet([twin, cross, across])
    here.make_parts(barrier, 3, send_part)
    low, mid, high = here.weights()

    def pass_on(step):
        hop(0, step).wait_recv()
        hop(2, step).start()
        hop(1, step).wait_recv()
        for e in range(half):
            for i in range(here.own_b):
                summed = low * here.part[step, half + e, i].astype(F32) + mid * got_away[step, e, i].astype(F32)
                mixed[step, e, i] = summed.astype(BF16)
        hop(3, step).start()

    def add_up(step):
        hop(2, step).wait_recv()
        hop(3, step).wait_recv()
        top(step).wait_recv()
        for e in range(half):
            for i in range(here.own_b):
                summed = low * got_first[step, e, i].astype(F32) + mid * got_on[step, e, i].astype(F32)
                summed = summed + high * got_top[step, e, i].astype(F32)
                here.total[step, e, i] = summed.astype(BF16)
                summed = got_sum[step, e, i].astype(F32) + high * got_top[step, half + e, i].astype(F32)
                here.total[step, half + e, i] = summed.astype(BF16)

    lag = min(LAG, steps)

    @pl.loop(0, lag)
    def _(step):
        pass_on(step)

    @pl.loop(lag, steps)
    def _(step):
        pass_on(step)
        add_up(step - lag)
        here.give(step - lag).start()

    @pl.loop(steps - lag, steps - 1)
    def _(step):
        add_up(step)
        here.give(step).start()

    add_up(steps - 1)
    here.keep().start()

    @pl.loop(0, steps)
    def _(step):
        for kind in range(4):
            hop(kind, step).wait_send()
        top(step).wait_send()

    here.finish()


def call(bits, n_atom, retarded, sigma_in, bit_shifts, occupation, neighbors, coupling):
    own_e, blocks, _, norb, _ = retarded.shape
    own_b = blocks // n_atom
    pieces = (n_atom, own_e, own_b, 2, norb, norb)
    halves = (n_atom, own_e // 2, own_b, 2, norb, norb)
    count = len(bits)
    smem = pl.BlockSpec(memory_space=pltpu.SMEM)
    hbm = pl.BlockSpec(memory_space=pl.ANY)
    dma = pltpu.SemaphoreType.DMA
    if bits[1] == 1:
        body = near_kernel
        extra = [pltpu.VMEM((count, *pieces), BF16), dma((count, n_atom)), dma((count, n_atom))]
    else:
        body = far_kernel
        extra = [pltpu.VMEM(halves, BF16) for _ in range(4)]
        extra += [pltpu.VMEM(pieces, BF16), pltpu.VMEM(halves, BF16)]
        extra += [dma((4, n_atom)), dma((4, n_atom)), dma((n_atom,)), dma((n_atom,))]
    return pl.pallas_call(
        functools.partial(body, bits, n_atom),
        out_shape=jax.ShapeDtypeStruct((own_e * n_atom, own_b, 2, norb, norb), BF16),
        in_specs=[smem, smem, smem, hbm, hbm, pl.BlockSpec(memory_space=pltpu.VMEM)],
        out_specs=hbm,
        scratch_shapes=[
            pltpu.VMEM(retarded.shape, BF16),
            pltpu.VMEM(retarded.shape, BF16),
            pltpu.VMEM(retarded.shape, BF16),
            pltpu.VMEM(pieces, BF16),
            pltpu.VMEM(pieces, BF16),
            dma((2, n_atom)),
            dma((n_atom,)),
            dma((n_atom,)),
            dma(()),
            *extra,
        ],
        compiler_params=pltpu.CompilerParams(
            collective_id=bits[1], has_side_effects=True, vmem_limit_bytes=50 * 2**20
        ),
        name="self_energy",
    )(bit_shifts, occupation, neighbors, retarded, sigma_in, coupling)


def on_device(retarded, sigma_in, bit_shifts, occupation, neighbors, coupling):
    n_atom = lax.axis_size("atom")
    top = lax.axis_size("win").bit_length() - 2
    return lax.cond(
        jnp.any(bit_shifts == 1),
        functools.partial(call, (0, 1, top), n_atom),
        functools.partial(call, (0, 2, top), n_atom),
        retarded,
        sigma_in,
        bit_shifts,
        occupation,
        neighbors,
        coupling,
    )


def solution(mesh):
    return jax.shard_map(
        on_device,
        mesh=mesh,
        in_specs=(
            P(("win", "atom"), None, None, None, None),
            P(("win", "atom"), None, None, None, None),
            P(),
            P(),
            P(),
            P(),
        ),
        out_specs=P("win", "atom", None, None, None),
        check_vma=False,
    )
```

time: 198 us -> 215 us (1.086)
  the two profiles are of different devices: /device:TPU:32 before, /device:TPU:25 now
where the time goes in v2:
time: 215 us
  Pallas kernels  210 us (98%)
  local copies, waits for them, and re-layouts  2.78 us (1%)
    pallas_call x1, Pallas kernels, call(): pl.pallas_call(functools.partial(body, bits, n_atom), out_shape=jax.Shape...  210 us

profile of v2, /device:TPU:25, one launch (start us, length us, event | category | flops | bytes accessed | tf_op | source)
XLA Modules:
  0.0 215.0 jit_solution(11079768175788289531)
XLA Ops:
  0.0 1.3 compare_reduce_fusion
  1.9 211.0 %conditional.1 = (bf16[32,2,2,128,128]{4,3,2,1,0:T(8,128)(2,1)S(1)}) conditional(s32[]{:T(128)} %convert_element_type.3, (s32[3]{0:T(128)}, f32[3]{0:T(128)}, s32[32,3]{0,1:T(4,128)}, bf16[2,32,2,128,128]{4,3,2,1,0:T(8,128)(2,1)}, bf16[2,32,2,128,128]{4,3,2,1,0:T(8,128)(2,1)}, /*index=5*/bf16[3,128,128]{2,1,0:T(8,128)(2,1)}) %tuple.11, (s32[3]{0:T(128)}, ...), branch_computations={%region_1.0_spmd, %region_2.0_spmd} | conditional | bytes 776 | solution.py:357
  2.0 0.8 copy.9.refs_2_
  2.7 210.2 %self_energy.2 = bf16[32,2,2,128,128]{4,3,2,1,0:T(8,128)(2,1)S(1)} custom-call(s32[3]{0:T(128)} %get-tuple-element.32.refs_0_, f32[3]{0:T(128)} %get-tuple-element.33.refs_1_, s32[32,3]{1,0:T(8,128)S(1)} %copy.9.refs_2_, bf16[2,32,2,128,128]{4,3,2,1,0:T(8,128)(2,1)} %get-tuple-element.35.refs_3_, bf16[2,32,2,128,128]{4,3,2,1,0:T(8,128)(2,1)} %get-tuple-element.36.refs_4_, ...), custom_call_target="tpu_custom_call" | custom-call | tf_op jit(solution)/shard_map/cond/branch_0_fun/self_energy/pallas_call | solution.py:330
  213.0 2.0 copy.14

commit v3 on v2

v3 whole, which is shorter than its diff:
```python
import functools

import jax
import jax.numpy as jnp
from jax import lax
from jax.experimental import pallas as pl
from jax.experimental.pallas import tpu as pltpu
from jax.sharding import PartitionSpec as P

MESH = pl.DeviceIdType.MESH
F32 = jnp.float32
BF16 = jnp.bfloat16
LAG = 3
STRIDE = 3


def dot(left, right, contract):
    return lax.dot_general(left, right, ((contract[0:1], contract[1:2]), ((), ())), preferred_element_type=F32)


def fold(quad, norb):
    real = quad[:norb, :norb] - quad[norb:, norb:]
    imag = quad[:norb, norb:] + quad[norb:, :norb]
    return jnp.concatenate([real, imag], axis=0).astype(BF16)


def flip(win, bit):
    mask = 2**bit
    return win + mask * (1 - 2 * ((win // mask) % 2))


class Context:
    def __init__(self, bits, n_atom, refs):
        (
            self.shifts_hbm,
            self.occ_hbm,
            self.near_hbm,
            self.green_hbm,
            self.sigma_hbm,
            self.coupling_hbm,
            self.out,
            self.shifts,
            self.occ,
            self.near,
            self.coupling,
            self.green,
            self.sigma,
            self.lesser,
            self.part,
            self.held,
            self.small_sem,
            self.in_sem,
            self.give_sem,
            self.take_sem,
        ) = refs
        self.bits = bits
        self.n_atom = n_atom
        self.own_e = self.green.shape[0]
        self.blocks = self.lesser.shape[1]
        self.own_b = self.blocks // n_atom
        self.norb = self.green.shape[-1]
        self.win = lax.axis_index("win")
        self.atom = lax.axis_index("atom")
        self.sign = 1 - 2 * (self.atom % 2)

    def owner(self, offset):
        return lax.rem(self.atom + offset, self.n_atom)

    def sent(self, turn):
        return lax.rem(self.sign * ((STRIDE * turn) % self.n_atom) + self.n_atom, self.n_atom)

    def met(self, turn):
        offset = (STRIDE * turn) % self.n_atom
        return lax.rem(self.sign * (1 - 2 * (offset % 2)) * offset + self.n_atom, self.n_atom)

    def block(self, place):
        return lax.rem(self.atom * self.own_b + place + self.blocks - 1, self.blocks)

    def small(self, which):
        source, target = (
            (self.near_hbm, self.near),
            (self.coupling_hbm, self.coupling),
            (self.shifts_hbm, self.shifts),
            (self.occ_hbm, self.occ),
        )[which]
        return pltpu.make_async_copy(source, target, self.small_sem.at[which])

    def load(self, kind, place):
        source, target = ((self.green_hbm, self.green), (self.sigma_hbm, self.sigma))[kind]
        b = self.block(place)
        return pltpu.make_async_copy(source.at[:, b], target.at[:, b], self.in_sem.at[kind, place])

    def start_loads(self, places):
        @pl.loop(*places)
        def _(place):
            self.load(0, place).start()
            self.load(1, place).start()

    def begin(self, partners):
        first = self.own_b + 2
        self.start_loads((0, first))
        for which in range(4):
            self.small(which).start()
        barrier = pltpu.get_barrier_semaphore()
        for partner in partners:
            pl.semaphore_signal(barrier, inc=1, device_id=(partner, self.atom), device_id_type=MESH)

        @pl.loop(1, self.n_atom)
        def _(i):
            pl.semaphore_signal(barrier, inc=1, device_id=(self.win, self.owner(i)), device_id_type=MESH)

        self.start_loads((first, self.blocks))
        for place in range(first):
            self.make_lesser(place)
        self.small(0).wait()
        self.small(1).wait()
        self.make_part(0, self.held)
        pl.semaphore_wait(barrier, len(partners) + self.n_atom - 1)

    def make_lesser(self, place):
        self.load(0, place).wait()
        self.load(1, place).wait()
        norb, b = self.norb, self.block(place)
        for e in range(self.own_e):
            g = self.green[e, b].reshape(2 * norb, norb)
            s = jnp.concatenate([self.sigma[e, b, 0], self.sigma[e, b, 1]], axis=1)
            product = fold(dot(g, s, (1, 0)), norb)
            self.lesser[e, b] = fold(dot(product, g, (1, 1)), norb).reshape(2, norb, norb)

    def make_part(self, step, target):
        norb, own_e = self.norb, self.own_e
        j = self.owner(step)
        matrices = [self.coupling[d] for d in range(self.coupling.shape[0])]
        for i in range(self.own_b):
            bent = []
            for d, matrix in enumerate(matrices):
                n = self.near[d, j * self.own_b + i]
                tiles = []
                for e in range(own_e):
                    picked = self.lesser[e, n]
                    tiles += [picked[0], picked[1]]
                wide = dot(matrix, jnp.concatenate(tiles, axis=1), (1, 0)).astype(BF16)
                bent.append(
                    jnp.concatenate([wide[:, t * norb : (t + 1) * norb] for t in range(2 * own_e)], axis=0)
                )
            full = dot(jnp.concatenate(bent, axis=1), jnp.concatenate(matrices, axis=1), (1, 1)).astype(BF16)
            for e in range(own_e):
                target[step, e, i] = full[2 * e * norb : 2 * (e + 1) * norb].reshape(2, norb, norb)

    def give(self, step):
        return pltpu.make_async_remote_copy(
            src_ref=self.part.at[step],
            dst_ref=self.held.at[step],
            send_sem=self.give_sem.at[step],
            recv_sem=self.take_sem.at[step],
            device_id=(self.win, self.owner(step)),
            device_id_type=MESH,
        )

    def make_parts(self, send):
        steps = self.n_atom
        lag = min(LAG, steps - 1)
        apart = self.sign * pow(STRIDE, -1, steps) + steps
        send(0)

        @pl.loop(1, steps)
        def _(turn):
            offset = self.sent(turn)

            @pl.when((turn + 2 * steps - apart) % steps > turn)
            def _():
                for i in range(self.own_b):
                    self.make_lesser(self.own_b * offset + i)

            @pl.when((turn + apart) % steps > turn)
            def _():
                for i in range(self.own_b):
                    self.make_lesser(self.own_b * (offset + 1) + i)

            self.make_part(offset, self.part)
            self.give(offset).start()

            @pl.when(turn > lag)
            def _():
                self.send_held(self.met(turn - lag), send)

        @pl.loop(steps - lag, steps)
        def _(turn):
            self.send_held(self.met(turn), send)

    def send_held(self, slot, send):
        self.give(slot).wait_recv()
        send(slot)

    def weights(self):
        self.small(2).wait()
        self.small(3).wait()
        weights = []
        for bit in self.bits:
            weight = jnp.float32(0.0)
            for mode in range(self.shifts.shape[0]):
                weight = weight + jnp.where(self.shifts[mode] == bit, self.occ[mode], 0.0)
            weights.append(weight)
        return weights

    def store(self, slot, e, i, value):
        sender = lax.rem(self.atom + self.n_atom - slot, self.n_atom)
        self.out[sender * self.own_e + e, i] = value.astype(BF16)

    def finish(self):
        @pl.loop(1, self.n_atom)
        def _(step):
            self.give(step).wait_send()


def near_kernel(bits, n_atom, *refs):
    here = Context(bits, n_atom, refs[:20])
    got, send_sem, recv_sem = refs[20:]
    partners = [flip(here.win, bit) for bit in bits]
    count = len(bits)

    def pass_to(k, slot):
        return pltpu.make_async_remote_copy(
            src_ref=here.held.at[slot],
            dst_ref=got.at[k, slot],
            send_sem=send_sem.at[k, slot],
            recv_sem=recv_sem.at[k, slot],
            device_id=(partners[k], here.atom),
            device_id_type=MESH,
        )

    def send(slot):
        for k in range(count):
            pass_to(k, slot).start()

    here.begin(partners)
    here.make_parts(send)
    weights = here.weights()

    @pl.loop(0, n_atom)
    def _(turn):
        slot = here.met(turn)
        for k in range(count):
            pass_to(k, slot).wait_recv()
        for e in range(here.own_e):
            for i in range(here.own_b):
                summed = weights[0] * got[0, slot, e, i].astype(F32)
                for k in range(1, count):
                    summed = summed + weights[k] * got[k, slot, e, i].astype(F32)
                here.store(slot, e, i, summed)

    @pl.loop(0, n_atom)
    def _(slot):
        for k in range(count):
            pass_to(k, slot).wait_send()

    here.finish()


def far_kernel(bits, n_atom, *refs):
    here = Context(bits, n_atom, refs[:20])
    got_first, got_away, got_on, got_sum, got_top, mixed, half_send, half_recv, top_send, top_recv = refs[20:]
    half = here.own_e // 2
    lead, rest = pl.ds(0, half), pl.ds(half, half)
    twin = flip(here.win, bits[0])
    cross = flip(twin, bits[1])
    across = flip(here.win, bits[2])

    def hop(kind, slot):
        source, target, win = (
            (here.held.at[slot, lead], got_first.at[slot], twin),
            (here.held.at[slot, rest], got_away.at[slot], cross),
            (got_first.at[slot], got_on.at[slot], cross),
            (mixed.at[slot], got_sum.at[slot], twin),
        )[kind]
        return pltpu.make_async_remote_copy(
            src_ref=source,
            dst_ref=target,
            send_sem=half_send.at[kind, slot],
            recv_sem=half_recv.at[kind, slot],
            device_id=(win, here.atom),
            device_id_type=MESH,
        )

    def top(slot):
        return pltpu.make_async_remote_copy(
            src_ref=here.held.at[slot],
            dst_ref=got_top.at[slot],
            send_sem=top_send.at[slot],
            recv_sem=top_recv.at[slot],
            device_id=(across, here.atom),
            device_id_type=MESH,
        )

    def send(slot):
        hop(0, slot).start()
        hop(1, slot).start()

    here.begin([twin, cross, across])
    here.make_parts(send)
    low, mid, high = here.weights()

    def pass_on(slot):
        hop(0, slot).wait_recv()
        hop(2, slot).start()
        top(slot).start()
        hop(1, slot).wait_recv()
        for e in range(half):
            for i in range(here.own_b):
                summed = low * here.held[slot, half + e, i].astype(F32) + mid * got_away[slot, e, i].astype(F32)
                mixed[slot, e, i] = summed.astype(BF16)
        hop(3, slot).start()

    @pl.loop(0, n_atom)
    def _(turn):
        pass_on(here.met(turn))

    @pl.loop(0, n_atom)
    def _(turn):
        slot = here.met(turn)
        hop(2, slot).wait_recv()
        hop(3, slot).wait_recv()
        top(slot).wait_recv()
        for e in range(half):
            for i in range(here.own_b):
                summed = low * got_first[slot, e, i].astype(F32) + mid * got_on[slot, e, i].astype(F32)
                here.store(slot, e, i, summed + high * got_top[slot, e, i].astype(F32))
                summed = got_sum[slot, e, i].astype(F32) + high * got_top[slot, half + e, i].astype(F32)
                here.store(slot, half + e, i, summed)

    @pl.loop(0, n_atom)
    def _(slot):
        for kind in range(4):
            hop(kind, slot).wait_send()
        top(slot).wait_send()

    here.finish()


def call(bits, n_atom, retarded, sigma_in, bit_shifts, occupation, neighbors, coupling):
    own_e, blocks, _, norb, _ = retarded.shape
    own_b = blocks // n_atom
    pieces = (n_atom, own_e, own_b, 2, norb, norb)
    halves = (n_atom, own_e // 2, own_b, 2, norb, norb)
    count = len(bits)
    dma = pltpu.SemaphoreType.DMA
    if bits[1] == 1:
        body = near_kernel
        extra = [pltpu.VMEM((count, *pieces), BF16), dma((count, n_atom)), dma((count, n_atom))]
    else:
        body = far_kernel
        extra = [pltpu.VMEM(halves, BF16) for _ in range(4)]
        extra += [pltpu.VMEM(pieces, BF16), pltpu.VMEM(halves, BF16)]
        extra += [dma((4, n_atom)), dma((4, n_atom)), dma((n_atom,)), dma((n_atom,))]
    return pl.pallas_call(
        functools.partial(body, bits, n_atom),
        out_shape=jax.ShapeDtypeStruct((own_e * n_atom, own_b, 2, norb, norb), BF16),
        in_specs=[pl.BlockSpec(memory_space=pl.ANY)] * 6,
        out_specs=pl.BlockSpec(memory_space=pltpu.VMEM),
        scratch_shapes=[
            pltpu.SMEM(bit_shifts.shape, jnp.int32),
            pltpu.SMEM(occupation.shape, F32),
            pltpu.SMEM(neighbors.shape[::-1], jnp.int32),
            pltpu.VMEM(coupling.shape, BF16),
            pltpu.VMEM(retarded.shape, BF16),
            pltpu.VMEM(retarded.shape, BF16),
            pltpu.VMEM(retarded.shape, BF16),
            pltpu.VMEM(pieces, BF16),
            pltpu.VMEM(pieces, BF16),
            dma((4,)),
            dma((2, blocks)),
            dma((n_atom,)),
            dma((n_atom,)),
            *extra,
        ],
        compiler_params=pltpu.CompilerParams(
            collective_id=bits[1], has_side_effects=True, vmem_limit_bytes=50 * 2**20
        ),
        name="self_energy",
    )(bit_shifts, occupation, neighbors.T, retarded, sigma_in, coupling)


def on_device(retarded, sigma_in, bit_shifts, occupation, neighbors, coupling):
    n_atom = lax.axis_size("atom")
    top = lax.axis_size("win").bit_length() - 2
    return lax.cond(
        jnp.any(bit_shifts == 1),
        functools.partial(call, (0, 1, top), n_atom),
        functools.partial(call, (0, 2, top), n_atom),
        retarded,
        sigma_in,
        bit_shifts,
        occupation,
        neighbors,
        coupling,
    )


def solution(mesh):
    return jax.shard_map(
        on_device,
        mesh=mesh,
        in_specs=(
            P(("win", "atom"), None, None, None, None),
            P(("win", "atom"), None, None, None, None),
            P(),
            P(),
            P(),
            P(),
        ),
        out_specs=P("win", "atom", None, None, None),
        check_vma=False,
    )
```

time: 215 us -> 195 us (0.907); the launches traced: 215 us -> 191 us
  Pallas kernels: 210 us -> 187 us
    pallas_call x1, Pallas kernels: 210 us -> 187 us  [call(): pl.pallas_call(functools.partial(body, bits, n_atom), out_shape=jax.Shape...]
where the time goes in v3:
time: 195 us; the launch traced here: 191 us
  Pallas kernels  187 us (96%)
  local copies, waits for them, and re-layouts  2.02 us (1%)
    pallas_call x1, Pallas kernels, call(): pl.pallas_call(functools.partial(body, bits, n_atom), out_shape=jax.Shape...  187 us

profile of v3, /device:TPU:25, one launch (start us, length us, event | category | flops | bytes accessed | tf_op | source)
XLA Modules:
  0.0 191.5 jit_solution(157697399991311152)
XLA Ops:
  0.0 1.3 compare_reduce_fusion
  1.9 187.5 %conditional.1 = (bf16[32,2,2,128,128]{4,3,2,1,0:T(8,128)(2,1)S(1)}) conditional(s32[]{:T(128)} %convert_element_type.3, (s32[32,3]{0,1:T(4,128)}, s32[3]{0:T(128)}, f32[3]{0:T(128)}, bf16[2,32,2,128,128]{4,3,2,1,0:T(8,128)(2,1)}, bf16[2,32,2,128,128]{4,3,2,1,0:T(8,128)(2,1)}, /*index=5*/bf16[3,128,128]{2,1,0:T(8,128)(2,1)}) %tuple.11, ...), branch_computations={%region_1.0_spmd, %region_2.0_spmd} | conditional | bytes 8 | solution.py:386
  2.0 187.5 %self_energy.3 = bf16[32,2,2,128,128]{4,3,2,1,0:T(8,128)(2,1)S(1)} custom-call(s32[3]{0:T(128)} %get-tuple-element.38.refs_0_, f32[3]{0:T(128)} %get-tuple-element.39.refs_1_, s32[3,32]{1,0:T(4,128)} %bitcast.3, bf16[2,32,2,128,128]{4,3,2,1,0:T(8,128)(2,1)} %get-tuple-element.41.refs_3_, bf16[2,32,2,128,128]{4,3,2,1,0:T(8,128)(2,1)} %get-tuple-element.42.refs_4_, ...), custom_call_target="tpu_custom_call" | custom-call | tf_op jit(solution)/shard_map/cond/branch_1_fun/self_energy/pallas_call | solution.py:355
  189.5 2.0 %copy.12 = bf16[32,2,2,128,128]{4,3,2,1,0:T(8,128)(2,1)} copy(bf16[32,2,2,128,128]{4,3,2,1,0:T(8,128)(2,1)S(1)} %get-tuple-element.44) | data formatting | bytes 8388608

commit v4 on v3

--- a/solution.py
+++ b/solution.py
@@ -10,7 +10,7 @@
 MESH = pl.DeviceIdType.MESH
 F32 = jnp.float32
 BF16 = jnp.bfloat16
-LAG = 3
+LAG = 2
 STRIDE = 3
 
 
@@ -66,12 +66,22 @@
     def owner(self, offset):
         return lax.rem(self.atom + offset, self.n_atom)
 
+    def swapped(self, value):
+        other = STRIDE % self.n_atom
+        return jnp.where(value == 1, other, jnp.where(value == other, 1, value))
+
+    def distance(self, turn):
+        return self.swapped((STRIDE * turn) % self.n_atom)
+
+    def turn_of(self, distance):
+        return (pow(STRIDE, -1, self.n_atom) * self.swapped(distance)) % self.n_atom
+
     def sent(self, turn):
-        return lax.rem(self.sign * ((STRIDE * turn) % self.n_atom) + self.n_atom, self.n_atom)
+        return lax.rem(self.sign * self.distance(turn) + self.n_atom, self.n_atom)
 
     def met(self, turn):
-        offset = (STRIDE * turn) % self.n_atom
-        return lax.rem(self.sign * (1 - 2 * (offset % 2)) * offset + self.n_atom, self.n_atom)
+        distance = self.distance(turn)
+        return lax.rem(self.sign * (1 - 2 * (distance % 2)) * distance + self.n_atom, self.n_atom)
 
     def block(self, place):
         return lax.rem(self.atom * self.own_b + place + self.blocks - 1, self.blocks)
@@ -96,7 +106,7 @@
             self.load(0, place).start()
             self.load(1, place).start()
 
-    def begin(self, partners):
+    def begin(self, partners, send):
         first = self.own_b + 2
         self.start_loads((0, first))
         for which in range(4):
@@ -109,13 +119,21 @@
         def _(i):
             pl.semaphore_signal(barrier, inc=1, device_id=(self.win, self.owner(i)), device_id_type=MESH)
 
-        self.start_loads((first, self.blocks))
+        early = self.n_atom > 2
+        forward = (self.sign + 1) // 2
+        if early:
+            start = self.own_b * (2 * forward + (self.n_atom - 1) * (1 - forward))
+            self.start_loads((start, start + self.own_b))
         for place in range(first):
             self.make_lesser(place)
         self.small(0).wait()
         self.small(1).wait()
         self.make_part(0, self.held)
         pl.semaphore_wait(barrier, len(partners) + self.n_atom - 1)
+        send(0)
+        if early:
+            start = first + self.own_b * forward
+            self.start_loads((start, start + self.blocks - first - self.own_b))
 
     def make_lesser(self, place):
         self.load(0, place).wait()
@@ -160,19 +178,20 @@
     def make_parts(self, send):
         steps = self.n_atom
         lag = min(LAG, steps - 1)
-        apart = self.sign * pow(STRIDE, -1, steps) + steps
-        send(0)
 
         @pl.loop(1, steps)
         def _(turn):
             offset = self.sent(turn)
 
-            @pl.when((turn + 2 * steps - apart) % steps > turn)
+            before = self.turn_of((self.distance(turn) + steps - self.sign) % steps)
+            after = self.turn_of((self.distance(turn) + steps + self.sign) % steps)
+
+            @pl.when(before > turn)
             def _():
                 for i in range(self.own_b):
                     self.make_lesser(self.own_b * offset + i)
 
-            @pl.when((turn + apart) % steps > turn)
+            @pl.when(after > turn)
             def _():
                 for i in range(self.own_b):
                     self.make_lesser(self.own_b * (offset + 1) + i)
@@ -180,7 +199,11 @@
             self.make_part(offset, self.part)
             self.give(offset).start()
 
-            @pl.when(turn > lag)
+            @pl.when(turn == 2)
+            def _():
+                self.send_held(self.met(1), send)
+
+            @pl.when(turn > lag + 1)
             def _():
                 self.send_held(self.met(turn - lag), send)
 
@@ -233,7 +256,7 @@
         for k in range(count):
             pass_to(k, slot).start()
 
-    here.begin(partners)
+    here.begin(partners, send)
     here.make_parts(send)
     weights = here.weights()
 
@@ -296,7 +319,7 @@
         hop(0, slot).start()
         hop(1, slot).start()
 
-    here.begin([twin, cross, across])
+    here.begin([twin, cross, across], send)
     here.make_parts(send)
     low, mid, high = here.weights()
 

time: 195 us -> 201 us (1.031)
  Pallas kernels: 187 us -> 195 us
    pallas_call x1, Pallas kernels: 187 us -> 195 us  [call(): pl.pallas_call(functools.partial(body, bits, n_atom), out_shape=jax.Shape...]
where the time goes in v4:
time: 201 us; the launch traced here: 199 us
  Pallas kernels  195 us (97%)
  local copies, waits for them, and re-layouts  2.02 us (1%)
    pallas_call x1, Pallas kernels, call(): pl.pallas_call(functools.partial(body, bits, n_atom), out_shape=jax.Shape...  195 us

profile of v4, /device:TPU:25, one launch (start us, length us, event | category | flops | bytes accessed | tf_op | source)
XLA Modules:
  0.0 198.7 jit_solution(6175704219726478248)
XLA Ops:
  0.0 1.3 compare_reduce_fusion
  1.9 194.8 %conditional.1 = (bf16[32,2,2,128,128]{4,3,2,1,0:T(8,128)(2,1)S(1)}) conditional(s32[]{:T(128)} %convert_element_type.3, (s32[32,3]{0,1:T(4,128)}, s32[3]{0:T(128)}, f32[3]{0:T(128)}, bf16[2,32,2,128,128]{4,3,2,1,0:T(8,128)(2,1)}, bf16[2,32,2,128,128]{4,3,2,1,0:T(8,128)(2,1)}, /*index=5*/bf16[3,128,128]{2,1,0:T(8,128)(2,1)}) %tuple.11, ...), branch_computations={%region_1.0_spmd, %region_2.0_spmd} | conditional | bytes 8 | solution.py:409
  2.0 194.8 %self_energy.2 = bf16[32,2,2,128,128]{4,3,2,1,0:T(8,128)(2,1)S(1)} custom-call(s32[3]{0:T(128)} %get-tuple-element.32.refs_0_, f32[3]{0:T(128)} %get-tuple-element.33.refs_1_, s32[3,32]{1,0:T(4,128)} %bitcast.2, bf16[2,32,2,128,128]{4,3,2,1,0:T(8,128)(2,1)} %get-tuple-element.35.refs_3_, bf16[2,32,2,128,128]{4,3,2,1,0:T(8,128)(2,1)} %get-tuple-element.36.refs_4_, ...), custom_call_target="tpu_custom_call" | custom-call | tf_op jit(solution)/shard_map/cond/branch_0_fun/self_energy/pallas_call | solution.py:378
  196.7 2.0 %copy.12 = bf16[32,2,2,128,128]{4,3,2,1,0:T(8,128)(2,1)} copy(bf16[32,2,2,128,128]{4,3,2,1,0:T(8,128)(2,1)S(1)} %get-tuple-element.44) | data formatting | bytes 8388608

commit v5 on v4

--- a/solution.py
+++ b/solution.py
@@ -230,10 +230,10 @@
         sender = lax.rem(self.atom + self.n_atom - slot, self.n_atom)
         self.out[sender * self.own_e + e, i] = value.astype(BF16)
 
-    def finish(self):
-        @pl.loop(1, self.n_atom)
-        def _(step):
-            self.give(step).wait_send()
+    def given(self, slot):
+        @pl.when(slot > 0)
+        def _():
+            self.give(slot).wait_send()
 
 
 def near_kernel(bits, n_atom, *refs):
@@ -263,21 +263,15 @@
     @pl.loop(0, n_atom)
     def _(turn):
         slot = here.met(turn)
+        here.given(slot)
         for k in range(count):
-            pass_to(k, slot).wait_recv()
+            pass_to(k, slot).wait()
         for e in range(here.own_e):
             for i in range(here.own_b):
                 summed = weights[0] * got[0, slot, e, i].astype(F32)
                 for k in range(1, count):
                     summed = summed + weights[k] * got[k, slot, e, i].astype(F32)
                 here.store(slot, e, i, summed)
-
-    @pl.loop(0, n_atom)
-    def _(slot):
-        for k in range(count):
-            pass_to(k, slot).wait_send()
-
-    here.finish()
 
 
 def far_kernel(bits, n_atom, *refs):
@@ -341,23 +335,18 @@
     @pl.loop(0, n_atom)
     def _(turn):
         slot = here.met(turn)
-        hop(2, slot).wait_recv()
-        hop(3, slot).wait_recv()
-        top(slot).wait_recv()
+        here.given(slot)
+        hop(0, slot).wait_send()
+        hop(1, slot).wait_send()
+        hop(2, slot).wait()
+        hop(3, slot).wait()
+        top(slot).wait()
         for e in range(half):
             for i in range(here.own_b):
                 summed = low * got_first[slot, e, i].astype(F32) + mid * got_on[slot, e, i].astype(F32)
                 here.store(slot, e, i, summed + high * got_top[slot, e, i].astype(F32))
                 summed = got_sum[slot, e, i].astype(F32) + high * got_top[slot, half + e, i].astype(F32)
                 here.store(slot, half + e, i, summed)
-
-    @pl.loop(0, n_atom)
-    def _(slot):
-        for kind in range(4):
-            hop(kind, slot).wait_send()
-        top(slot).wait_send()
-
-    here.finish()
 
 
 def call(bits, n_atom, retarded, sigma_in, bit_shifts, occupation, neighbors, coupling):

time: 201 us -> 198 us (0.985); the launches traced: 199 us -> 198 us
  no operation moved by 1% of the time
where the time goes in v5:
time: 198 us
  Pallas kernels  194 us (98%)
  local copies, waits for them, and re-layouts  2.02 us (1%)
    pallas_call x1, Pallas kernels, call(): pl.pallas_call(functools.partial(body, bits, n_atom), out_shape=jax.Shape...  194 us

profile of v5, /device:TPU:25, one launch (start us, length us, event | category | flops | bytes accessed | tf_op | source)
XLA Modules:
  0.0 198.5 jit_solution(153805524847509840)
XLA Ops:
  0.0 1.3 compare_reduce_fusion
  1.9 194.5 %conditional.1 = (bf16[32,2,2,128,128]{4,3,2,1,0:T(8,128)(2,1)S(1)}) conditional(s32[]{:T(128)} %convert_element_type.3, (s32[32,3]{0,1:T(4,128)}, s32[3]{0:T(128)}, f32[3]{0:T(128)}, bf16[2,32,2,128,128]{4,3,2,1,0:T(8,128)(2,1)}, bf16[2,32,2,128,128]{4,3,2,1,0:T(8,128)(2,1)}, /*index=5*/bf16[3,128,128]{2,1,0:T(8,128)(2,1)}) %tuple.11, ...), branch_computations={%region_1.0_spmd, %region_2.0_spmd} | conditional | bytes 8 | solution.py:398
  2.0 194.5 %self_energy.2 = bf16[32,2,2,128,128]{4,3,2,1,0:T(8,128)(2,1)S(1)} custom-call(s32[3]{0:T(128)} %get-tuple-element.32.refs_0_, f32[3]{0:T(128)} %get-tuple-element.33.refs_1_, s32[3,32]{1,0:T(4,128)} %bitcast.2, bf16[2,32,2,128,128]{4,3,2,1,0:T(8,128)(2,1)} %get-tuple-element.35.refs_3_, bf16[2,32,2,128,128]{4,3,2,1,0:T(8,128)(2,1)} %get-tuple-element.36.refs_4_, ...), custom_call_target="tpu_custom_call" | custom-call | tf_op jit(solution)/shard_map/cond/branch_0_fun/self_energy/pallas_call | solution.py:367
  196.5 2.0 %copy.12 = bf16[32,2,2,128,128]{4,3,2,1,0:T(8,128)(2,1)} copy(bf16[32,2,2,128,128]{4,3,2,1,0:T(8,128)(2,1)S(1)} %get-tuple-element.44) | data formatting | bytes 8388608

commit v6 on v5

--- a/solution.py
+++ b/solution.py
@@ -11,7 +11,7 @@
 F32 = jnp.float32
 BF16 = jnp.bfloat16
 LAG = 2
-STRIDE = 3
+STRIDE = 11
 
 
 def dot(left, right, contract):

time: 198 us -> 197 us (level); the launches traced: 198 us -> 194 us
  Pallas kernels: 194 us -> 190 us
    pallas_call x1, Pallas kernels: 194 us -> 190 us  [call(): pl.pallas_call(functools.partial(body, bits, n_atom), out_shape=jax.Shape...]
where the time goes in v6:
time: 197 us; the launch traced here: 194 us
  Pallas kernels  190 us (96%)
  local copies, waits for them, and re-layouts  2.02 us (1%)
    pallas_call x1, Pallas kernels, call(): pl.pallas_call(functools.partial(body, bits, n_atom), out_shape=jax.Shape...  190 us

profile of v6, /device:TPU:25, one launch (start us, length us, event | category | flops | bytes accessed | tf_op | source)
XLA Modules:
  0.0 194.5 jit_solution(5875792683472806442)
XLA Ops:
  0.0 1.3 compare_reduce_fusion
  1.9 190.5 %conditional.1 = (bf16[32,2,2,128,128]{4,3,2,1,0:T(8,128)(2,1)S(1)}) conditional(s32[]{:T(128)} %convert_element_type.3, (s32[32,3]{0,1:T(4,128)}, s32[3]{0:T(128)}, f32[3]{0:T(128)}, bf16[2,32,2,128,128]{4,3,2,1,0:T(8,128)(2,1)}, bf16[2,32,2,128,128]{4,3,2,1,0:T(8,128)(2,1)}, /*index=5*/bf16[3,128,128]{2,1,0:T(8,128)(2,1)}) %tuple.11, ...), branch_computations={%region_1.0_spmd, %region_2.0_spmd} | conditional | bytes 8 | solution.py:398
  2.0 190.5 %self_energy.2 = bf16[32,2,2,128,128]{4,3,2,1,0:T(8,128)(2,1)S(1)} custom-call(s32[3]{0:T(128)} %get-tuple-element.32.refs_0_, f32[3]{0:T(128)} %get-tuple-element.33.refs_1_, s32[3,32]{1,0:T(4,128)} %bitcast.2, bf16[2,32,2,128,128]{4,3,2,1,0:T(8,128)(2,1)} %get-tuple-element.35.refs_3_, bf16[2,32,2,128,128]{4,3,2,1,0:T(8,128)(2,1)} %get-tuple-element.36.refs_4_, ...), custom_call_target="tpu_custom_call" | custom-call | tf_op jit(solution)/shard_map/cond/branch_0_fun/self_energy/pallas_call | solution.py:367
  192.5 2.0 %copy.12 = bf16[32,2,2,128,128]{4,3,2,1,0:T(8,128)(2,1)} copy(bf16[32,2,2,128,128]{4,3,2,1,0:T(8,128)(2,1)S(1)} %get-tuple-element.44) | data formatting | bytes 8388608
